TPU v7x, 128 devices: a whole 4x4x4 slice. The times are simulated.
128 devices in a mesh: blk: 64 (over z, y, x_lo, core), rep: 2 (over x_hi).
Axes of the slice: x: 4 (x_hi: 2, x_lo: 2; x = x_hi * 2 + x_lo), y: 4, z: 4, core: 2. Of those that a mesh axis runs over, the one named last changes fastest.
Arguments:
- examples: float32 [32768, 1024], P(('blk', 'rep')), may hold values from -6 to 6
- targets: float32 [32768, 1000], P(('blk', 'rep')), may hold values from -6 to 6
- hop_reach: int32 [32768], P(('blk', 'rep')), may hold values from 1 to 5
- centers: float32 [16384, 1024], P('blk'), may hold values from -6 to 6
- coeffs: float32 [16384, 1000], P('blk'), may hold values from -0.15625 to 0.15625
- step_gain: float32 [16384], P('blk'), may hold values from 0.5 to 2
Outputs:
- new_coeffs: float32 [16384, 1000], P('blk')
- residual: float32 [32768, 1000], P(('blk', 'rep'))
All inputs are finite; a program needn't handle non-finite values.
Results may differ from a plain program's by a relative error of at most 0.0003.
Values sent between devices are 32-bit elements; how exact they have to be, the bound alone decides.
A program may use at most 64 MiB of HBM per device.

v0:
```python
import math

import jax
import jax.numpy as jnp
from jax import lax
from jax.sharding import PartitionSpec as P

HOPS = 4


def passed_along(block, axis, distance):
    devices = range(lax.axis_size(axis))
    route = [((i - distance) % len(devices), i) for i in devices]
    return lax.ppermute(block, axis, route)


def from_everyone(shard, axis):
    copies = jnp.broadcast_to(shard, (lax.axis_size(axis), *shard.shape))
    return lax.all_to_all(copies, axis, split_axis=0, concat_axis=0, tiled=True)


def taken_together(shard, axis):
    return from_everyone(shard, axis).sum(axis=0)


def on_device(examples, targets, hop_reach, centers, coeffs, step_gain):
    sharpness = 0.5 / math.sqrt(examples.shape[1])
    blocks = [(centers, coeffs)]
    current = (centers, coeffs)
    for distance in range(1, HOPS + 1):
        current = passed_along((current[0], current[1]), "blk", 1)
        blocks.append(current)
    kernels = []
    predicted = jnp.zeros(targets.shape, jnp.float32)
    for distance in range(HOPS + 1):
        block_centers = blocks[distance][0]
        scores = lax.dot_general(
            examples,
            block_centers,
            (((1,), (1,)), ((), ())),
            precision=lax.Precision.HIGHEST,
            preferred_element_type=jnp.float32,
        )
        visible = (hop_reach > distance).astype(jnp.float32)[:, None]
        kernel = jnp.exp(sharpness * scores) * visible
        kernels.append(kernel)
        predicted = predicted + jnp.dot(
            kernel,
            blocks[distance][1],
            precision=lax.Precision.HIGHEST,
            preferred_element_type=jnp.float32,
        )
    residual = predicted - targets

    def contribution(distance):
        return lax.dot_general(
            kernels[distance],
            residual,
            (((0,), (0,)), ((), ())),
            precision=lax.Precision.HIGHEST,
            preferred_element_type=jnp.float32,
        )

    accumulated = jnp.zeros(coeffs.shape, jnp.float32)
    for distance in range(HOPS, 0, -1):
        accumulated = accumulated + contribution(distance)
        accumulated = passed_along(accumulated, "blk", -1)
    accumulated = accumulated + contribution(0)
    gradient = taken_together(accumulated, "rep")
    step_size = 1.0 / math.sqrt(examples.shape[0] * lax.axis_size("rep") * (HOPS + 1))
    new_coeffs = coeffs - (step_size * step_gain)[:, None] * gradient
    return (new_coeffs, residual)


def solution(mesh):
    in_specs = (
        P(("blk", "rep"), None),
        P(("blk", "rep"), None),
        P(("blk", "rep")),
        P("blk", None),
        P("blk", None),
        P("blk"),
    )
    out_specs = (P("blk", None), P(("blk", "rep"), None))
    return jax.shard_map(
        on_device, mesh=mesh, in_specs=in_specs, out_specs=out_specs, check_vma=False
    )
```

profile of v0, /device:TPU:0, one launch (start us, length us, event | category | flops | bytes accessed | tf_op | source)
XLA Modules:
  0.0 203.0 jit_solution(2747486825573193721)
XLA Ops:
  0.7 1.7 collective-permute-start.4
  2.4 17.9 %collective-permute-done = f32[256,1024]{1,0:T(8,128)S(1)} collective-permute-done((f32[256,1024]{1,0:T(8,128)}, f32[256,1024]{1,0:T(8,128)S(1)}, u32[]{:S(2)}, u32[]{:S(2)}) %collective-permute-start) | collective-permute-done | bytes 1048608 | tf_op jit(solution)/shard_map/ppermute | solution.py:14
  20.4 11.0 %collective-permute-done.4 = f32[256,1000]{0,1:T(8,128)S(1)} collective-permute-done((f32[256,1000]{0,1:T(8,128)}, f32[256,1000]{0,1:T(8,128)S(1)}, u32[]{:S(2)}, u32[]{:S(2)}) %collective-permute-start.4) | collective-permute-done | bytes 1024032 | tf_op jit(solution)/shard_map/ppermute | solution.py:14
  32.0 10.5 %collective-permute-done.1 = f32[256,1024]{1,0:T(8,128)S(1)} collective-permute-done((f32[256,1024]{1,0:T(8,128)S(1)}, f32[256,1024]{1,0:T(8,128)S(1)}, u32[]{:S(2)}, u32[]{:S(2)}) %collective-permute-start.1) | collective-permute-done | bytes 1048608 | tf_op jit(solution)/shard_map/ppermute | solution.py:14
  42.6 2.3 %fusion.8 = f32[256,256]{1,0:T(8,128)S(1)} fusion(f32[256,1024]{1,0:T(8,128)S(1)} %copy-done, f32[256,1024]{1,0:T(8,128)} %param.9, f32[256]{0:T(256)S(1)} %get-tuple-element.4), kind=kOutput, calls=%fused_computation.17 | convolution fusion | flops 805437440 | bytes 2360320 | tf_op jit(solution)/shard_map/dot_general | solution.py:37
  44.8 8.7 %collective-permute-done.5 = f32[256,1000]{0,1:T(8,128)S(1)} collective-permute-done((f32[256,1000]{0,1:T(8,128)S(1)}, f32[256,1000]{0,1:T(8,128)S(1)}, u32[]{:S(2)}, u32[]{:S(2)}) %collective-permute-start.5) | collective-permute-done | bytes 1024032 | tf_op jit(solution)/shard_map/ppermute | solution.py:14
  56.6 8.1 %collective-permute-done.2 = f32[256,1024]{1,0:T(8,128)S(1)} collective-permute-done((f32[256,1024]{1,0:T(8,128)S(1)}, f32[256,1024]{1,0:T(8,128)S(1)}, u32[]{:S(2)}, u32[]{:S(2)}) %collective-permute-start.2) | collective-permute-done | bytes 1048608 | tf_op jit(solution)/shard_map/ppermute | solution.py:14
  65.8 9.9 %collective-permute-done.6 = f32[256,1000]{0,1:T(8,128)S(1)} collective-permute-done((f32[256,1000]{0,1:T(8,128)S(1)}, f32[256,1000]{0,1:T(8,128)S(1)}, u32[]{:S(2)}, u32[]{:S(2)}) %collective-permute-start.6) | collective-permute-done | bytes 1024032 | tf_op jit(solution)/shard_map/ppermute | solution.py:14
  78.9 8.1 %collective-permute-done.3 = f32[256,1024]{1,0:T(8,128)S(1)} collective-permute-done((f32[256,1024]{1,0:T(8,128)S(1)}, f32[256,1024]{1,0:T(8,128)S(1)}, u32[]{:S(2)}, u32[]{:S(2)}) %collective-permute-start.3) | collective-permute-done | bytes 1048608 | tf_op jit(solution)/shard_map/ppermute | solution.py:14
  88.0 9.9 %collective-permute-done.7 = f32[256,1000]{0,1:T(8,128)S(1)} collective-permute-done((f32[256,1000]{0,1:T(8,128)S(1)}, f32[256,1000]{0,1:T(8,128)S(1)}, u32[]{:S(2)}, u32[]{:S(2)}) %collective-permute-start.7) | collective-permute-done | bytes 1024032 | tf_op jit(solution)/shard_map/ppermute | solution.py:14
  98.0 1.1 fusion
  100.1 12.0 %collective-permute-done.8 = f32[256,1000]{0,1:T(8,128)S(1)} collective-permute-done((f32[256,1000]{0,1:T(8,128)S(1)}, f32[256,1000]{0,1:T(8,128)S(1)}, u32[]{:S(2)}, u32[]{:S(2)}) %collective-permute-start.8) | collective-permute-done | bytes 1024032 | tf_op jit(solution)/shard_map/ppermute | solution.py:14
  112.2 1.1 convolution_add_fusion
  113.2 6.2 %collective-permute-start.9 = (f32[256,1000]{0,1:T(8,128)S(1)}, f32[256,1000]{0,1:T(8,128)S(1)}, u32[]{:S(2)}, u32[]{:S(2)}) collective-permute-start(f32[256,1000]{0,1:T(8,128)S(1)} %convolution_add_fusion), channel_id=1, source_target_pairs={{2,0},{4,2},{6,4},{8,6},{10,8},{12,10},{14,12},{16,14},{18,16},{20... | collective-permute-start | bytes 3072008 | tf_op jit(solution)/shard_map/ppermute | solution.py:14
  120.4 11.0 %collective-permute-done.9 = f32[256,1000]{0,1:T(8,128)S(1)} collective-permute-done((f32[256,1000]{0,1:T(8,128)S(1)}, f32[256,1000]{0,1:T(8,128)S(1)}, u32[]{:S(2)}, u32[]{:S(2)}) %collective-permute-start.9) | collective-permute-done | bytes 1024032 | tf_op jit(solution)/shard_map/ppermute | solution.py:14
  131.6 6.2 %collective-permute-start.10 = (f32[256,1000]{0,1:T(8,128)S(1)}, f32[256,1000]{0,1:T(8,128)S(1)}, u32[]{:S(2)}, u32[]{:S(2)}) collective-permute-start(f32[256,1000]{0,1:T(8,128)S(1)} %add.29), channel_id=1, source_target_pairs={{2,0},{4,2},{6,4},{8,6},{10,8},{12,10},{14,12},{16,14},{18,16},{20... | collective-permute-start | bytes 3072008 | tf_op jit(solution)/shard_map/ppermute | solution.py:14
  138.8 11.0 %collective-permute-done.10 = f32[256,1000]{0,1:T(8,128)S(1)} collective-permute-done((f32[256,1000]{0,1:T(8,128)S(1)}, f32[256,1000]{0,1:T(8,128)S(1)}, u32[]{:S(2)}, u32[]{:S(2)}) %collective-permute-start.10) | collective-permute-done | bytes 1024032 | tf_op jit(solution)/shard_map/ppermute | solution.py:14
  150.0 6.2 %collective-permute-start.11 = (f32[256,1000]{0,1:T(8,128)S(1)}, f32[256,1000]{0,1:T(8,128)S(1)}, u32[]{:S(2)}, u32[]{:S(2)}) collective-permute-start(f32[256,1000]{0,1:T(8,128)S(1)} %add.30), channel_id=1, source_target_pairs={{2,0},{4,2},{6,4},{8,6},{10,8},{12,10},{14,12},{16,14},{18,16},{20... | collective-permute-start | bytes 3072008 | tf_op jit(solution)/shard_map/ppermute | solution.py:14
  157.2 20.3 %collective-permute-done.11 = f32[256,1000]{0,1:T(8,128)S(1)} collective-permute-done((f32[256,1000]{0,1:T(8,128)S(1)}, f32[256,1000]{0,1:T(8,128)S(1)}, u32[]{:S(2)}, u32[]{:S(2)}) %collective-permute-start.11) | collective-permute-done | bytes 1024032 | tf_op jit(solution)/shard_map/ppermute | solution.py:14
  177.6 1.5 broadcast_in_dim.2
  179.1 3.9 %all-to-all-start = ((f32[2,256,1000]{1,2,0:T(8,128)}), f32[2,256,1000]{1,2,0:T(8,128)S(1)}, u32[]{:S(2)}, u32[]{:S(2)}) async-start(f32[2,256,1000]{1,2,0:T(8,128)} %broadcast_in_dim.2), calls=%async_computation | async-start | bytes 4096000 | tf_op jit(solution)/shard_map/all_to_all | solution.py:19
  183.0 16.2 %all-to-all-done = f32[2,256,1000]{1,2,0:T(8,128)S(1)} async-done(((f32[2,256,1000]{1,2,0:T(8,128)}), f32[2,256,1000]{1,2,0:T(8,128)S(1)}, u32[]{:S(2)}, u32[]{:S(2)}) %all-to-all-start) | async-done | bytes 2048032 | tf_op jit(solution)/shard_map/all_to_all | solution.py:19
  199.2 1.2 reduce_sum.9
  200.4 2.6 %multiply_subtract_fusion = f32[256,1000]{0,1:T(8,128)} fusion(f32[256,1000]{0,1:T(8,128)} %param.10, f32[256,1000]{0,1:T(8,128)} %reduce_sum.9, f32[256]{0:T(256)S(1)} %broadcast_multiply_fusion), kind=kLoop, calls=%fused_computation.21 | loop fusion | flops 512000 | bytes 3073024 | tf_op jit(solution)/shard_map/sub | solution.py:71
  (35 shorter events, 13.5 us)
Async XLA Ops:
  0.6 41.9 %copy-start = (f32[256,1024]{1,0:T(8,128)S(1)}, f32[256,1024]{1,0:T(8,128)}, u32[]{:S(2)}) copy-start(f32[256,1024]{1,0:T(8,128)} %param.6) | copy-start | bytes 3145732
  0.6 52.9 %copy-start.2 = (f32[256,1000]{0,1:T(8,128)S(1)}, f32[256,1000]{0,1:T(8,128)}, u32[]{:S(2)}) copy-start(f32[256,1000]{0,1:T(8,128)} %param.10) | copy-start | bytes 3072004
  0.7 19.7 %collective-permute-start = (f32[256,1024]{1,0:T(8,128)}, f32[256,1024]{1,0:T(8,128)S(1)}, u32[]{:S(2)}, u32[]{:S(2)}) collective-permute-start(f32[256,1024]{1,0:T(8,128)} %param.9), channel_id=1, source_target_pairs={{126,0},{0,2},{2,4},{4,6},{6,8},{8,10},{10,12},{12,14},{14,16},{16... | collective-permute-start | bytes 3145736 | tf_op jit(solution)/shard_map/ppermute | solution.py:14
  0.7 30.6 %collective-permute-start.4 = (f32[256,1000]{0,1:T(8,128)}, f32[256,1000]{0,1:T(8,128)S(1)}, u32[]{:S(2)}, u32[]{:S(2)}) collective-permute-start(f32[256,1000]{0,1:T(8,128)} %param.10), channel_id=1, source_target_pairs={{126,0},{0,2},{2,4},{4,6},{6,8},{8,10},{10,12},{12,14},{14,16},{16... | collective-permute-start | bytes 3072008 | tf_op jit(solution)/shard_map/ppermute | solution.py:14
  20.4 22.2 %collective-permute-start.1 = (f32[256,1024]{1,0:T(8,128)S(1)}, f32[256,1024]{1,0:T(8,128)S(1)}, u32[]{:S(2)}, u32[]{:S(2)}) collective-permute-start(f32[256,1024]{1,0:T(8,128)S(1)} %collective-permute-done), channel_id=1, source_target_pairs={{126,0},{0,2},{2,4},{4,6},{6,8},{8,10},{10,12},{12,14},{14,16},{16... | collective-permute-start | bytes 3145736 | tf_op jit(solution)/shard_map/ppermute | solution.py:14
  31.3 22.2 %collective-permute-start.5 = (f32[256,1000]{0,1:T(8,128)S(1)}, f32[256,1000]{0,1:T(8,128)S(1)}, u32[]{:S(2)}, u32[]{:S(2)}) collective-permute-start(f32[256,1000]{0,1:T(8,128)S(1)} %collective-permute-done.4), channel_id=1, source_target_pairs={{126,0},{0,2},{2,4},{4,6},{6,8},{8,10},{10,12},{12,14},{14,16},{16... | collective-permute-start | bytes 3072008 | tf_op jit(solution)/shard_map/ppermute | solution.py:14
  42.6 22.2 %collective-permute-start.2 = (f32[256,1024]{1,0:T(8,128)S(1)}, f32[256,1024]{1,0:T(8,128)S(1)}, u32[]{:S(2)}, u32[]{:S(2)}) collective-permute-start(f32[256,1024]{1,0:T(8,128)S(1)} %collective-permute-done.1), channel_id=1, source_target_pairs={{126,0},{0,2},{2,4},{4,6},{6,8},{8,10},{10,12},{12,14},{14,16},{16... | collective-permute-start | bytes 3145736 | tf_op jit(solution)/shard_map/ppermute | solution.py:14
  53.5 22.2 %collective-permute-start.6 = (f32[256,1000]{0,1:T(8,128)S(1)}, f32[256,1000]{0,1:T(8,128)S(1)}, u32[]{:S(2)}, u32[]{:S(2)}) collective-permute-start(f32[256,1000]{0,1:T(8,128)S(1)} %collective-permute-done.5), channel_id=1, source_target_pairs={{126,0},{0,2},{2,4},{4,6},{6,8},{8,10},{10,12},{12,14},{14,16},{16... | collective-permute-start | bytes 3072008 | tf_op jit(solution)/shard_map/ppermute | solution.py:14
  64.8 22.2 %collective-permute-start.3 = (f32[256,1024]{1,0:T(8,128)S(1)}, f32[256,1024]{1,0:T(8,128)S(1)}, u32[]{:S(2)}, u32[]{:S(2)}) collective-permute-start(f32[256,1024]{1,0:T(8,128)S(1)} %collective-permute-done.2), channel_id=1, source_target_pairs={{126,0},{0,2},{2,4},{4,6},{6,8},{8,10},{10,12},{12,14},{14,16},{16... | collective-permute-start | bytes 3145736 | tf_op jit(solution)/shard_map/ppermute | solution.py:14
  75.7 22.2 %collective-permute-start.7 = (f32[256,1000]{0,1:T(8,128)S(1)}, f32[256,1000]{0,1:T(8,128)S(1)}, u32[]{:S(2)}, u32[]{:S(2)}) collective-permute-start(f32[256,1000]{0,1:T(8,128)S(1)} %collective-permute-done.6), channel_id=1, source_target_pairs={{126,0},{0,2},{2,4},{4,6},{6,8},{8,10},{10,12},{12,14},{14,16},{16... | collective-permute-start | bytes 3072008 | tf_op jit(solution)/shard_map/ppermute | solution.py:14
  77.8 20.1 %copy-start.3 = (f32[256,1000]{0,1:T(8,128)S(1)}, f32[256,1000]{0,1:T(8,128)}, u32[]{:S(2)}) copy-start(f32[256,1000]{0,1:T(8,128)} %param.7) | copy-start | bytes 3072004
  99.0 57.2 %copy-start.1 = (f32[256,1000]{0,1:T(8,128)}, f32[256,1000]{0,1:T(8,128)S(1)}, u32[]{:S(2)}) copy-start(f32[256,1000]{0,1:T(8,128)S(1)} %fusion) | copy-start | bytes 3072004
  100.0 12.1 %collective-permute-start.8 = (f32[256,1000]{0,1:T(8,128)S(1)}, f32[256,1000]{0,1:T(8,128)S(1)}, u32[]{:S(2)}, u32[]{:S(2)}) collective-permute-start(f32[256,1000]{0,1:T(8,128)S(1)} %fusion.12), channel_id=1, source_target_pairs={{2,0},{4,2},{6,4},{8,6},{10,8},{12,10},{14,12},{16,14},{18,16},{20... | collective-permute-start | bytes 3072008 | tf_op jit(solution)/shard_map/ppermute | solution.py:14
  113.2 18.3 %collective-permute-start.9 = (f32[256,1000]{0,1:T(8,128)S(1)}, f32[256,1000]{0,1:T(8,128)S(1)}, u32[]{:S(2)}, u32[]{:S(2)}) collective-permute-start(f32[256,1000]{0,1:T(8,128)S(1)} %convolution_add_fusion), channel_id=1, source_target_pairs={{2,0},{4,2},{6,4},{8,6},{10,8},{12,10},{14,12},{16,14},{18,16},{20... | collective-permute-start | bytes 3072008 | tf_op jit(solution)/shard_map/ppermute | solution.py:14
  131.6 18.2 %collective-permute-start.10 = (f32[256,1000]{0,1:T(8,128)S(1)}, f32[256,1000]{0,1:T(8,128)S(1)}, u32[]{:S(2)}, u32[]{:S(2)}) collective-permute-start(f32[256,1000]{0,1:T(8,128)S(1)} %add.29), channel_id=1, source_target_pairs={{2,0},{4,2},{6,4},{8,6},{10,8},{12,10},{14,12},{16,14},{18,16},{20... | collective-permute-start | bytes 3072008 | tf_op jit(solution)/shard_map/ppermute | solution.py:14
  150.0 27.5 %collective-permute-start.11 = (f32[256,1000]{0,1:T(8,128)S(1)}, f32[256,1000]{0,1:T(8,128)S(1)}, u32[]{:S(2)}, u32[]{:S(2)}) collective-permute-start(f32[256,1000]{0,1:T(8,128)S(1)} %add.30), channel_id=1, source_target_pairs={{2,0},{4,2},{6,4},{8,6},{10,8},{12,10},{14,12},{16,14},{18,16},{20... | collective-permute-start | bytes 3072008 | tf_op jit(solution)/shard_map/ppermute | solution.py:14
  179.1 3.9 %copy-start.4 = (f32[256]{0:T(256)S(1)}, f32[256]{0:T(256)}, u32[]{:S(2)}) copy-start(f32[256]{0:T(256)} %param.11) | copy-start | bytes 3076
  179.1 20.1 %all-to-all-start = ((f32[2,256,1000]{1,2,0:T(8,128)}), f32[2,256,1000]{1,2,0:T(8,128)S(1)}, u32[]{:S(2)}, u32[]{:S(2)}) async-start(f32[2,256,1000]{1,2,0:T(8,128)} %broadcast_in_dim.2), calls=%async_computation | async-start | bytes 4096000 | tf_op jit(solution)/shard_map/all_to_all | solution.py:19
where the time goes:
time: 203 us
  waiting for transfers between devices  155 us (76%)
  starting transfers between devices  24.3 us (12%)
  matrix products  16.6 us (8%)
  other arithmetic  4.87 us (2%)
    ppermute x12, waiting for transfers between devices, passed_along(): return lax.ppermute(block, axis, route)  139 us
    ppermute x12, starting transfers between devices, passed_along(): return lax.ppermute(block, axis, route)  20.4 us
    all_to_all x1, waiting for transfers between devices, from_everyone(): return lax.all_to_all(copies, axis, split_axis=0, concat_axis=0, tiled=True)  16.2 us
    dot_general x5, matrix products, on_device(): lax.dot_general(examples, block_centers, (((1,), (1,)), ((), ())), precis...  6.45 us
    dot_general x5, matrix products, on_device(): jnp.dot(kernel, blocks[distance][1], precision=lax.Precision.HIGHEST, pre...  5.13 us
    dot_general x5, matrix products, contribution(): lax.dot_general(kernels[distance], residual, (((0,), (0,)), ((), ())), pr...  5.04 us
  transfers between devices with their start and end apart: 13, of which 13 were waited for; matrix products, arithmetic and copies ran while one was open for 7% of the time, Pallas kernels for 0%

commit v1 on v0

v1 whole, which is shorter than its diff:
```python
import functools
import math

import jax
import jax.numpy as jnp
from jax import lax
from jax.experimental import pallas as pl
from jax.experimental.pallas import tpu as pltpu
from jax.sharding import PartitionSpec as P

HOPS = 4
MESH = pl.DeviceIdType.MESH
HIGHEST = lax.Precision.HIGHEST
OWN, D, X, PY, PX = range(5)
NT = (((1,), (1,)), ((), ()))
NN = (((1,), (0,)), ((), ()))


def spans(sizes):
    out, at = [], 0
    for size in sizes:
        out.append((at, size))
        at += size
    return out


def kernel(
    cpieces, wpieces, sharpness,
    ex_hbm, tgt_hbm, hop_ref, cen_hbm, cof_hbm, scale_ref,
    newc_hbm, res_hbm,
    cbuf, wbuf, ex, tgt, kt, res, grad, gsend, rpy, rpx, rx, ry, re, newc,
    d_s, d_r, xa_s, xa_r, xb_s, xb_r, py_s, py_r, px_s, px_r,
    gpy_s, gpy_r, gpx_s, gpx_r, gx_s, gx_r, gy_s, gy_r, ge_s, ge_r,
    load_sem, out_sem,
):
    b = lax.axis_index("blk")
    r = lax.axis_index("rep")
    n_blk = lax.axis_size("blk")
    q = lax.rem(b, 4)
    xl = q // 2
    core = lax.rem(q, 2)
    base = b - q
    is_l = xl == 0
    is_h = xl == 1
    up = (lax.rem(b + 4, n_blk), r)
    down = (lax.rem(b + n_blk - 4, n_blk), r)
    near = base + (1 - xl) * 2 + core
    x1 = (near, r)
    x3 = (near, 1 - r)
    x2 = (b, 1 - r)
    peer = (base + xl * 2 + 1 - core, r)

    def load(i, src, dst):
        return pltpu.make_async_copy(src, dst, load_sem.at[i])

    loads = [
        load(0, cen_hbm, cbuf.at[OWN]),
        load(1, cof_hbm, wbuf.at[OWN]),
        load(2, ex_hbm, ex),
        load(3, tgt_hbm, tgt),
    ]
    for copy in loads:
        copy.start()

    barrier = pltpu.get_barrier_semaphore()
    for other in (up, down, x1, x3, x2, peer):
        pl.semaphore_signal(barrier, inc=1, device_id=other, device_id_type=MESH)
    pl.semaphore_wait(barrier, 6)

    nc, nw = len(cpieces), len(wpieces)
    n = nc + nw

    def part(i, slot):
        if i < nc:
            lo, size = cpieces[i]
            return cbuf.at[slot, pl.ds(lo, size)]
        lo, size = wpieces[i - nc]
        return wbuf.at[slot, pl.ds(lo, size)]

    def cut(i):
        if i < nc:
            lo, size = cpieces[i]
            return cbuf, lo, size // 2, size
        lo, size = wpieces[i - nc]
        return wbuf, lo, 0, size

    def remote(src, dst, ssem, rsem, to):
        return pltpu.make_async_remote_copy(
            src_ref=src, dst_ref=dst, send_sem=ssem, recv_sem=rsem,
            device_id=to, device_id_type=MESH,
        )

    def d_copy(i):
        return remote(part(i, OWN), part(i, D), d_s.at[i], d_r.at[i], up)

    def x_copies(i):
        buf, lo, near_rows, size = cut(i)
        out = []
        if near_rows:
            span = pl.ds(lo, near_rows)
            out.append(remote(buf.at[xl, span], buf.at[X, span], xa_s.at[i], xa_r.at[i], x1))
        span = pl.ds(lo + near_rows, size - near_rows)
        out.append(remote(buf.at[xl, span], buf.at[X, span], xb_s.at[i], xb_r.at[i], x3))
        return out

    def py_copy(i):
        return remote(part(i, core), part(i, PY), py_s.at[i], py_r.at[i], peer)

    def px_copy(i):
        return remote(part(i, X), part(i, PX), px_s.at[i], px_r.at[i], peer)

    def rows(j):
        lo, size = wpieces[j]
        return pl.ds(lo, size)

    def gpy_copy(j):
        return remote(gsend.at[0, rows(j)], rpy.at[rows(j)], gpy_s.at[j], gpy_r.at[j], peer)

    def gpx_copy(j):
        return remote(gsend.at[1, rows(j)], rpx.at[rows(j)], gpx_s.at[j], gpx_r.at[j], peer)

    def gx_copy(j):
        return remote(grad.at[X, rows(j)], rx.at[rows(j)], gx_s.at[j], gx_r.at[j], x1)

    def gy_copy(j):
        return remote(grad.at[D, rows(j)], ry.at[rows(j)], gy_s.at[j], gy_r.at[j], down)

    def ge_copy(j):
        return remote(grad.at[OWN, rows(j)], re.at[rows(j)], ge_s.at[j], ge_r.at[j], x2)

    hop_of = {OWN: 0, D: 4, X: 2, PY: 3 - 2 * core, PX: 1 + 2 * core}

    def scores(slot, lo, size):
        products = lax.dot_general(
            cbuf[slot, lo:lo + size, :], ex[...], NT,
            precision=HIGHEST, preferred_element_type=jnp.float32,
        )
        visible = (hop_ref[...] > hop_of[slot]).astype(jnp.float32)
        kt[slot, lo:lo + size, :] = jnp.exp(sharpness * products) * visible

    def arrive(i):
        d_copy(i).wait_recv()

        @pl.when(is_h)
        def _():
            for copy in x_copies(i):
                copy.start()

        @pl.when(core == 1)
        def _():
            py_copy(i).start()

        d_copy(i).wait_send()
        if i + 2 < n:
            d_copy(i + 2).start()
        if i + nc < n:
            @pl.when(is_l)
            def _():
                for copy in x_copies(i + nc):
                    copy.start()

    def spread(i):
        for copy in x_copies(i):
            copy.wait_recv()
        px_copy(i).start()

    def ready(i):
        py_copy(i).wait_recv()
        px_copy(i).wait_recv()

    def contract(j):
        ready(nc + j)
        lo, size = wpieces[j]
        hi = lo + size
        total = -tgt[lo:hi, :]
        for slot in (OWN, D, X, PY, PX):
            total = total + lax.dot_general(
                wbuf[slot, lo:hi, :], kt[slot], NN,
                precision=HIGHEST, preferred_element_type=jnp.float32,
            )
        res[lo:hi, :] = total

        def term(slot):
            return lax.dot_general(
                res[lo:hi, :], kt[slot], NT,
                precision=HIGHEST, preferred_element_type=jnp.float32,
            )

        gsend[1, lo:hi, :] = term(PX)
        gpx_copy(j).start()
        gsend[0, lo:hi, :] = term(PY)
        gpy_copy(j).start()
        for slot in (X, D, OWN):
            grad[slot, lo:hi, :] = term(slot)
        out_copy(0, j).start()

    def out_copy(which, j):
        src, dst = ((res, res_hbm), (newc, newc_hbm))[which]
        return pltpu.make_async_copy(src.at[rows(j)], dst.at[rows(j)], out_sem.at[which, j])

    def fold(j):
        lo, size = wpieces[j]
        hi = lo + size
        gpx_copy(j).wait_recv()
        grad[X, lo:hi, :] = grad[X, lo:hi, :] + rpx[lo:hi, :]
        gx_copy(j).start()
        gpy_copy(j).wait_recv()

        @pl.when(core == 0)
        def _():
            grad[OWN, lo:hi, :] = grad[OWN, lo:hi, :] + rpy[lo:hi, :]

        @pl.when(core == 1)
        def _():
            grad[D, lo:hi, :] = grad[D, lo:hi, :] + rpy[lo:hi, :]

        @pl.when(is_l)
        def _():
            gy_copy(j).start()

    def descend(j):
        lo, size = wpieces[j]
        hi = lo + size
        gx_copy(j).wait_recv()

        @pl.when(is_h)
        def _():
            grad[D, lo:hi, :] = grad[D, lo:hi, :] + rx[lo:hi, :]
            gy_copy(j).start()

        @pl.when(is_l)
        def _():
            grad[OWN, lo:hi, :] = grad[OWN, lo:hi, :] + rx[lo:hi, :]

    def home(j):
        lo, size = wpieces[j]
        hi = lo + size
        gy_copy(j).wait_recv()
        grad[OWN, lo:hi, :] = grad[OWN, lo:hi, :] + ry[lo:hi, :]
        ge_copy(j).start()

    def finish(j):
        lo, size = wpieces[j]
        hi = lo + size
        ge_copy(j).wait_recv()
        total = grad[OWN, lo:hi, :] + re[lo:hi, :]
        newc[lo:hi, :] = wbuf[OWN, lo:hi, :] - scale_ref[...] * total
        out_copy(1, j).start()

    loads[0].wait()
    d_copy(0).start()
    d_copy(1).start()

    @pl.when(is_l)
    def _():
        for i in range(nc):
            for copy in x_copies(i):
                copy.start()

    loads[1].wait()

    @pl.when(core == 0)
    def _():
        for i in range(n):
            py_copy(i).start()

    loads[2].wait()
    scores(OWN, 0, cbuf.shape[1])
    loads[3].wait()

    def in_range(j):
        return 0 <= j < nw

    for k in range(n + 6):
        if k < n:
            arrive(k)
        if k < nc:
            scores(D, *cpieces[k])
        if 0 <= k - 1 < n:
            spread(k - 1)
        j = k - nc
        if in_range(j - 5):
            finish(j - 5)
        if in_range(j - 4):
            home(j - 4)
        if in_range(j - 3):
            descend(j - 3)
        if in_range(j - 2):
            fold(j - 2)
        if 0 <= k - 1 < nc:
            i = k - 1
            ready(i)
            for slot in (X, PY, PX):
                scores(slot, *cpieces[i])
        if in_range(j - 1):
            contract(j - 1)

    for i in range(n):
        for copy in x_copies(i):
            copy.wait_send()
        py_copy(i).wait_send()
        px_copy(i).wait_send()
    for j in range(nw):
        for make in (gpy_copy, gpx_copy, gx_copy, gy_copy, ge_copy):
            make(j).wait_send()
        out_copy(0, j).wait()
        out_copy(1, j).wait()


def on_device(examples, targets, hop_reach, centers, coeffs, step_gain):
    n_ex, width = examples.shape
    n_cen, n_out = coeffs.shape
    sharpness = 0.5 / math.sqrt(width)
    step_size = 1.0 / math.sqrt(n_ex * lax.axis_size("rep") * (HOPS + 1))
    cpieces = spans([n_cen // 4] * 4)
    wpieces = spans([n_out // 5] * 5)
    nc, nw = len(cpieces), len(wpieces)
    n = nc + nw
    f32 = jnp.float32
    whole = pl.BlockSpec(memory_space=pl.ANY)
    vmem = pl.BlockSpec(memory_space=pltpu.VMEM)
    dma = pltpu.SemaphoreType.DMA
    out = jax.ShapeDtypeStruct((n_out, n_cen), f32)
    flops = 4 * (HOPS + 1) * n_ex * n_cen * (width + 2 * n_out)
    new_coeffs, residual = pl.pallas_call(
        functools.partial(kernel, cpieces, wpieces, sharpness),
        out_shape=(out, jax.ShapeDtypeStruct((n_out, n_ex), f32)),
        in_specs=[whole, whole, vmem, whole, whole, vmem],
        out_specs=(whole, whole),
        scratch_shapes=[
            pltpu.VMEM((5, n_cen, width), f32),
            pltpu.VMEM((5, n_out, n_cen), f32),
            pltpu.VMEM((n_ex, width), f32),
            pltpu.VMEM((n_out, n_ex), f32),
            pltpu.VMEM((5, n_cen, n_ex), f32),
            pltpu.VMEM((n_out, n_ex), f32),
            pltpu.VMEM((3, n_out, n_cen), f32),
            pltpu.VMEM((2, n_out, n_cen), f32),
        ]
        + [pltpu.VMEM((n_out, n_cen), f32)] * 6
        + [dma((n,))] * 10
        + [dma((nw,))] * 10
        + [dma((4,)), dma((2, nw))],
        compiler_params=pltpu.CompilerParams(
            collective_id=0, has_side_effects=True, vmem_limit_bytes=56 * 2**20
        ),
        cost_estimate=pl.CostEstimate(
            flops=flops, bytes_accessed=7 * 4 * n_out * n_cen, transcendentals=0
        ),
    )(
        examples, targets.T, hop_reach[None, :], centers, coeffs.T,
        (step_size * step_gain)[None, :],
    )
    return (new_coeffs.T, residual.T)


def solution(mesh):
    in_specs = (
        P(("blk", "rep"), None),
        P(("blk", "rep"), None),
        P(("blk", "rep")),
        P("blk", None),
        P("blk", None),
        P("blk"),
    )
    out_specs = (P("blk", None), P(("blk", "rep"), None))
    return jax.shard_map(
        on_device, mesh=mesh, in_specs=in_specs, out_specs=out_specs, check_vma=False
    )
```

time: 203 us -> 112 us (0.55)
  waiting for transfers between devices: 155 us -> 0 us
  Pallas kernels: 0 us -> 107 us
  starting transfers between devices: 24.3 us -> 0 us
  matrix products: 16.6 us -> 0 us
  other arithmetic: 4.87 us -> 0.56 us
  local copies, waits for them, and re-layouts: 1.5 us -> 3.96 us
    ppermute x12 -> x0, waiting for transfers between devices: 139 us -> none  [passed_along(): return lax.ppermute(block, axis, route)]
    pallas_call x0 -> x1, Pallas kernels: none -> 107 us  [on_device(): pl.pallas_call(functools.partial(kernel, cpieces, wpieces, sharpness), ou...]
    ppermute x12 -> x0, starting transfers between devices: 20.4 us -> none  [passed_along(): return lax.ppermute(block, axis, route)]
    dot_general x15 -> x0, matrix products: 16.6 us -> none  [the longest x5 6.45 us: on_device(): lax.dot_general(examples, block_centers, (((1,), (1,)), ((), ())), precis...]
    all_to_all x1 -> x0, waiting for transfers between devices: 16.2 us -> none  [from_everyone(): return lax.all_to_all(copies, axis, split_axis=0, concat_axis=0, tiled=True)]
    unnamed x10 -> x6, local copies, waits for them, and re-layouts: 0.03 us -> 3.96 us
    all_to_all x1 -> x0, starting transfers between devices: 3.89 us -> none  [from_everyone(): return lax.all_to_all(copies, axis, split_axis=0, concat_axis=0, tiled=True)]
    sub x1 -> x0, other arithmetic: 2.61 us -> none  [on_device(): new_coeffs = coeffs - (step_size * step_gain)[:, None] * gradient]
  transfers between devices with their start and end apart: 13 -> 0, of which waited for: 13 -> 0; matrix products, arithmetic and copies ran while one was open for 7% -> 0% of each run, Pallas kernels for 0% -> 0%
where the time goes in v1:
time: 112 us
  Pallas kernels  107 us (96%)
  local copies, waits for them, and re-layouts  3.96 us (4%)
    pallas_call x1, Pallas kernels, on_device(): pl.pallas_call(functools.partial(kernel, cpieces, wpieces, sharpness), ou...  107 us
    unnamed x6, local copies, waits for them, and re-layouts  3.96 us

profile of v1, /device:TPU:0, one launch (start us, length us, event | category | flops | bytes accessed | tf_op | source)
XLA Modules:
  0.0 111.9 jit_solution(17574494508401859938)
XLA Ops:
  0.6 0.0 copy-start.1
  0.6 0.7 copy-done.1
  1.3 0.6 broadcast_multiply_fusion
  1.9 106.7 %shard_map.77 = (f32[1000,256]{1,0:T(8,128)}, f32[1000,256]{1,0:T(8,128)}) custom-call(f32[256,1024]{1,0:T(8,128)} %ex_hbm.1, f32[1000,256]{1,0:T(8,128)} %bitcast.9, s32[1,256]{1,0:T(1,128)} %bitcast.11, f32[256,1024]{1,0:T(8,128)} %cen_hbm.1, f32[1000,256]{1,0:T(8,128)} %bitcast.10, f32[1,256]{1,0:T(1,128)} %bitcast.8), custom_call_target="tpu_custom_call" | custom-call | flops 3963617280 | bytes 7168000 | tf_op jit(solution)/shard_map/pallas_call | solution.py:325
  108.6 0.0 copy-start
  108.6 2.3 %copy.10 = f32[256,1000]{0,1:T(8,128)} copy(f32[256,1000]{0,1:T(8,128)} %bitcast.7) | data formatting | bytes 2048000
  110.9 0.0 copy-done
  111.0 1.0 copy.11
Async XLA Ops:
  0.6 0.7 copy-start.1
  108.6 2.3 %copy-start = (f32[1000,256]{1,0:T(8,128)S(1)}, f32[1000,256]{1,0:T(8,128)}, u32[]{:S(2)}) copy-start(f32[1000,256]{1,0:T(8,128)} %get-tuple-element.5) | copy-start | bytes 3072004

commit v2 on v1

--- a/solution.py
+++ b/solution.py
@@ -10,7 +10,6 @@
 
 HOPS = 4
 MESH = pl.DeviceIdType.MESH
-HIGHEST = lax.Precision.HIGHEST
 OWN, D, X, PY, PX = range(5)
 NT = (((1,), (1,)), ((), ()))
 NN = (((1,), (0,)), ((), ()))
@@ -24,13 +23,33 @@
     return out
 
 
+def halves(a):
+    hi = a.astype(jnp.bfloat16)
+    lo = (a - hi.astype(jnp.float32)).astype(jnp.bfloat16)
+    return hi, lo
+
+
+def product(a, b_hi, b_lo, dims):
+    m = a.shape[0]
+    a_hi, a_lo = halves(a)
+    both = lax.dot_general(
+        jnp.concatenate([a_hi, a_lo]), b_hi, dims, preferred_element_type=jnp.float32
+    )
+    cross = lax.dot_general(a_hi, b_lo, dims, preferred_element_type=jnp.float32)
+    return both[:m] + (both[m:] + cross)
+
+
+def near_share(size):
+    return size // 16 * 8
+
+
 def kernel(
-    cpieces, wpieces, sharpness,
-    ex_hbm, tgt_hbm, hop_ref, cen_hbm, cof_hbm, scale_ref,
+    cpieces, wpieces, sharpness, step_size,
+    ex_hbm, tgt_hbm, hop_ref, cen_hbm, cof_hbm, gain_ref,
     newc_hbm, res_hbm,
-    cbuf, wbuf, ex, tgt, kt, res, grad, gsend, rpy, rpx, rx, ry, re, newc,
+    cbuf, wbuf, ex, ex2, tgt, kt, res, grad, gsend, rpy, rpx, rx, ry, re, newc,
     d_s, d_r, xa_s, xa_r, xb_s, xb_r, py_s, py_r, px_s, px_r,
-    gpy_s, gpy_r, gpx_s, gpx_r, gx_s, gx_r, gy_s, gy_r, ge_s, ge_r,
+    gpy_s, gpy_r, gpx_s, gpx_r, gxa_s, gxa_r, gxb_s, gxb_r, gy_s, gy_r, ge_s, ge_r,
     load_sem, out_sem,
 ):
     b = lax.axis_index("blk")
@@ -80,9 +99,9 @@
     def cut(i):
         if i < nc:
             lo, size = cpieces[i]
-            return cbuf, lo, size // 2, size
+            return cbuf, lo, near_share(size), size
         lo, size = wpieces[i - nc]
-        return wbuf, lo, 0, size
+        return wbuf, lo, near_share(size), size
 
     def remote(src, dst, ssem, rsem, to):
         return pltpu.make_async_remote_copy(
@@ -95,13 +114,11 @@
 
     def x_copies(i):
         buf, lo, near_rows, size = cut(i)
-        out = []
-        if near_rows:
-            span = pl.ds(lo, near_rows)
-            out.append(remote(buf.at[xl, span], buf.at[X, span], xa_s.at[i], xa_r.at[i], x1))
-        span = pl.ds(lo + near_rows, size - near_rows)
-        out.append(remote(buf.at[xl, span], buf.at[X, span], xb_s.at[i], xb_r.at[i], x3))
-        return out
+        one, two = pl.ds(lo, near_rows), pl.ds(lo + near_rows, size - near_rows)
+        return (
+            remote(buf.at[xl, one], buf.at[X, one], xa_s.at[i], xa_r.at[i], x1),
+            remote(buf.at[xl, two], buf.at[X, two], xb_s.at[i], xb_r.at[i], x3),
+        )
 
     def py_copy(i):
         return remote(part(i, core), part(i, PY), py_s.at[i], py_r.at[i], peer)
@@ -119,8 +136,14 @@
     def gpx_copy(j):
         return remote(gsend.at[1, rows(j)], rpx.at[rows(j)], gpx_s.at[j], gpx_r.at[j], peer)
 
-    def gx_copy(j):
-        return remote(grad.at[X, rows(j)], rx.at[rows(j)], gx_s.at[j], gx_r.at[j], x1)
+    def gx_copies(j):
+        lo, size = wpieces[j]
+        near_rows = near_share(size)
+        one, two = pl.ds(lo, near_rows), pl.ds(lo + near_rows, size - near_rows)
+        return (
+            remote(grad.at[X, one], rx.at[one], gxa_s.at[j], gxa_r.at[j], x1),
+            remote(grad.at[X, two], rx.at[two], gxb_s.at[j], gxb_r.at[j], x3),
+        )
 
     def gy_copy(j):
         return remote(grad.at[D, rows(j)], ry.at[rows(j)], gy_s.at[j], gy_r.at[j], down)
@@ -131,12 +154,10 @@
     hop_of = {OWN: 0, D: 4, X: 2, PY: 3 - 2 * core, PX: 1 + 2 * core}
 
     def scores(slot, lo, size):
-        products = lax.dot_general(
-            cbuf[slot, lo:lo + size, :], ex[...], NT,
-            precision=HIGHEST, preferred_element_type=jnp.float32,
-        )
+        products = product(cbuf[slot, lo:lo + size, :], ex2[0], ex2[1], NT)
         visible = (hop_ref[...] > hop_of[slot]).astype(jnp.float32)
-        kt[slot, lo:lo + size, :] = jnp.exp(sharpness * products) * visible
+        values = jnp.exp(sharpness * products) * visible
+        kt[0, slot, lo:lo + size, :], kt[1, slot, lo:lo + size, :] = halves(values)
 
     def arrive(i):
         d_copy(i).wait_recv()
@@ -151,8 +172,8 @@
             py_copy(i).start()
 
         d_copy(i).wait_send()
-        if i + 2 < n:
-            d_copy(i + 2).start()
+        if i + 3 < n:
+            d_copy(i + 3).start()
         if i + nc < n:
             @pl.when(is_l)
             def _():
@@ -174,17 +195,11 @@
         hi = lo + size
         total = -tgt[lo:hi, :]
         for slot in (OWN, D, X, PY, PX):
-            total = total + lax.dot_general(
-                wbuf[slot, lo:hi, :], kt[slot], NN,
-                precision=HIGHEST, preferred_element_type=jnp.float32,
-            )
+            total = total + product(wbuf[slot, lo:hi, :], kt[0, slot], kt[1, slot], NN)
         res[lo:hi, :] = total
 
         def term(slot):
-            return lax.dot_general(
-                res[lo:hi, :], kt[slot], NT,
-                precision=HIGHEST, preferred_element_type=jnp.float32,
-            )
+            return product(res[lo:hi, :], kt[0, slot], kt[1, slot], NT)
 
         gsend[1, lo:hi, :] = term(PX)
         gpx_copy(j).start()
@@ -203,7 +218,8 @@
         hi = lo + size
         gpx_copy(j).wait_recv()
         grad[X, lo:hi, :] = grad[X, lo:hi, :] + rpx[lo:hi, :]
-        gx_copy(j).start()
+        for copy in gx_copies(j):
+            copy.start()
         gpy_copy(j).wait_recv()
 
         @pl.when(core == 0)
@@ -221,7 +237,8 @@
     def descend(j):
         lo, size = wpieces[j]
         hi = lo + size
-        gx_copy(j).wait_recv()
+        for copy in gx_copies(j):
+            copy.wait_recv()
 
         @pl.when(is_h)
         def _():
@@ -244,12 +261,13 @@
         hi = lo + size
         ge_copy(j).wait_recv()
         total = grad[OWN, lo:hi, :] + re[lo:hi, :]
-        newc[lo:hi, :] = wbuf[OWN, lo:hi, :] - scale_ref[...] * total
+        newc[lo:hi, :] = wbuf[OWN, lo:hi, :] - (step_size * gain_ref[...]) * total
         out_copy(1, j).start()
 
     loads[0].wait()
     d_copy(0).start()
     d_copy(1).start()
+    d_copy(2).start()
 
     @pl.when(is_l)
     def _():
@@ -265,35 +283,36 @@
             py_copy(i).start()
 
     loads[2].wait()
+    ex2[0], ex2[1] = halves(ex[...])
     scores(OWN, 0, cbuf.shape[1])
     loads[3].wait()
 
     def in_range(j):
         return 0 <= j < nw
 
-    for k in range(n + 6):
-        if k < n:
-            arrive(k)
-        if k < nc:
-            scores(D, *cpieces[k])
-        if 0 <= k - 1 < n:
-            spread(k - 1)
-        j = k - nc
-        if in_range(j - 5):
-            finish(j - 5)
-        if in_range(j - 4):
-            home(j - 4)
+    for i in range(nc):
+        arrive(i)
+        scores(D, *cpieces[i])
+        spread(i)
+        ready(i)
+        for slot in (X, PY, PX):
+            scores(slot, *cpieces[i])
+    arrive(nc)
+    for j in range(nw + 3):
+        if in_range(j):
+            spread(nc + j)
+        if in_range(j + 1):
+            arrive(nc + j + 1)
+        if in_range(j):
+            contract(j)
+        if in_range(j - 1):
+            descend(j - 1)
+        if in_range(j):
+            fold(j)
+        if in_range(j - 2):
+            home(j - 2)
         if in_range(j - 3):
-            descend(j - 3)
-        if in_range(j - 2):
-            fold(j - 2)
-        if 0 <= k - 1 < nc:
-            i = k - 1
-            ready(i)
-            for slot in (X, PY, PX):
-                scores(slot, *cpieces[i])
-        if in_range(j - 1):
-            contract(j - 1)
+            finish(j - 3)
 
     for i in range(n):
         for copy in x_copies(i):
@@ -301,7 +320,9 @@
         py_copy(i).wait_send()
         px_copy(i).wait_send()
     for j in range(nw):
-        for make in (gpy_copy, gpx_copy, gx_copy, gy_copy, ge_copy):
+        for copy in gx_copies(j):
+            copy.wait_send()
+        for make in (gpy_copy, gpx_copy, gy_copy, ge_copy):
             make(j).wait_send()
         out_copy(0, j).wait()
         out_copy(1, j).wait()
@@ -313,7 +334,7 @@
     sharpness = 0.5 / math.sqrt(width)
     step_size = 1.0 / math.sqrt(n_ex * lax.axis_size("rep") * (HOPS + 1))
     cpieces = spans([n_cen // 4] * 4)
-    wpieces = spans([n_out // 5] * 5)
+    wpieces = spans([104,208,208,208,144,128])
     nc, nw = len(cpieces), len(wpieces)
     n = nc + nw
     f32 = jnp.float32
@@ -323,7 +344,7 @@
     out = jax.ShapeDtypeStruct((n_out, n_cen), f32)
     flops = 4 * (HOPS + 1) * n_ex * n_cen * (width + 2 * n_out)
     new_coeffs, residual = pl.pallas_call(
-        functools.partial(kernel, cpieces, wpieces, sharpness),
+        functools.partial(kernel, cpieces, wpieces, sharpness, step_size),
         out_shape=(out, jax.ShapeDtypeStruct((n_out, n_ex), f32)),
         in_specs=[whole, whole, vmem, whole, whole, vmem],
         out_specs=(whole, whole),
@@ -331,15 +352,16 @@
             pltpu.VMEM((5, n_cen, width), f32),
             pltpu.VMEM((5, n_out, n_cen), f32),
             pltpu.VMEM((n_ex, width), f32),
+            pltpu.VMEM((2, n_ex, width), jnp.bfloat16),
             pltpu.VMEM((n_out, n_ex), f32),
-            pltpu.VMEM((5, n_cen, n_ex), f32),
+            pltpu.VMEM((2, 5, n_cen, n_ex), jnp.bfloat16),
             pltpu.VMEM((n_out, n_ex), f32),
             pltpu.VMEM((3, n_out, n_cen), f32),
             pltpu.VMEM((2, n_out, n_cen), f32),
         ]
         + [pltpu.VMEM((n_out, n_cen), f32)] * 6
         + [dma((n,))] * 10
-        + [dma((nw,))] * 10
+        + [dma((nw,))] * 12
         + [dma((4,)), dma((2, nw))],
         compiler_params=pltpu.CompilerParams(
             collective_id=0, has_side_effects=True, vmem_limit_bytes=56 * 2**20
@@ -348,8 +370,7 @@
             flops=flops, bytes_accessed=7 * 4 * n_out * n_cen, transcendentals=0
         ),
     )(
-        examples, targets.T, hop_reach[None, :], centers, coeffs.T,
-        (step_size * step_gain)[None, :],
+        examples, targets.T, hop_reach[None, :], centers, coeffs.T, step_gain[None, :],
     )
     return (new_coeffs.T, residual.T)
 

time: 112 us -> 99.1 us (0.88)
  Pallas kernels: 107 us -> 95 us
    pallas_call x1, Pallas kernels: 107 us -> 95 us  [on_device(): pl.pallas_call(functools.partial(kernel, cpieces, wpieces, sharpness, ste...]
    unnamed x6 -> x4, local copies, waits for them, and re-layouts: 3.96 us -> 3.29 us
where the time goes in v2:
time: 99.1 us; the launch traced here: 99 us
  Pallas kernels  95 us (96%)
  local copies, waits for them, and re-layouts  3.29 us (3%)
    pallas_call x1, Pallas kernels, on_device(): pl.pallas_call(functools.partial(kernel, cpieces, wpieces, sharpness, ste...  95 us
    unnamed x4, local copies, waits for them, and re-layouts  3.29 us

profile of v2, /device:TPU:0, one launch (start us, length us, event | category | flops | bytes accessed | tf_op | source)
XLA Modules:
  0.0 99.0 jit_solution(5471273833525214658)
XLA Ops:
  0.6 95.0 %shard_map.77 = (f32[1000,256]{1,0:T(8,128)}, f32[1000,256]{1,0:T(8,128)}) custom-call(f32[256,1024]{1,0:T(8,128)} %ex_hbm.1, f32[1000,256]{1,0:T(8,128)} %bitcast.8, s32[1,256]{1,0:T(1,128)} %bitcast.10, f32[256,1024]{1,0:T(8,128)} %cen_hbm.1, f32[1000,256]{1,0:T(8,128)} %bitcast.9, f32[1,256]{1,0:T(1,128)} %bitcast.11), custom_call_target="tpu_custom_call" | custom-call | flops 3963617280 | bytes 7168000 | tf_op jit(solution)/shard_map/pallas_call | solution.py:346
  95.7 0.0 copy-start
  95.7 2.3 %copy.10 = f32[256,1000]{0,1:T(8,128)} copy(f32[256,1000]{0,1:T(8,128)} %bitcast.7) | data formatting | bytes 2048000
  98.0 0.0 copy-done
  98.0 1.0 copy.11
Async XLA Ops:
  95.7 2.3 %copy-start = (f32[1000,256]{1,0:T(8,128)S(1)}, f32[1000,256]{1,0:T(8,128)}, u32[]{:S(2)}) copy-start(f32[1000,256]{1,0:T(8,128)} %get-tuple-element.5) | copy-start | bytes 3072004

commit v3 on v2

--- a/solution.py
+++ b/solution.py
@@ -48,7 +48,7 @@
     ex_hbm, tgt_hbm, hop_ref, cen_hbm, cof_hbm, gain_ref,
     newc_hbm, res_hbm,
     cbuf, wbuf, ex, ex2, tgt, kt, res, grad, gsend, rpy, rpx, rx, ry, re, newc,
-    d_s, d_r, xa_s, xa_r, xb_s, xb_r, py_s, py_r, px_s, px_r,
+    d_s, d_r, e_s, e_r, xa_s, xa_r, xb_s, xb_r, py_s, py_r, px_s, px_r,
     gpy_s, gpy_r, gpx_s, gpx_r, gxa_s, gxa_r, gxb_s, gxb_r, gy_s, gy_r, ge_s, ge_r,
     load_sem, out_sem,
 ):
@@ -99,9 +99,11 @@
     def cut(i):
         if i < nc:
             lo, size = cpieces[i]
-            return cbuf, lo, near_share(size), size
+            half = pl.ds(lo + size // 2 * r, size // 2)
+            return cbuf, half, half
         lo, size = wpieces[i - nc]
-        return wbuf, lo, near_share(size), size
+        near_rows = near_share(size)
+        return wbuf, pl.ds(lo, near_rows), pl.ds(lo + near_rows, size - near_rows)
 
     def remote(src, dst, ssem, rsem, to):
         return pltpu.make_async_remote_copy(
@@ -110,11 +112,19 @@
         )
 
     def d_copy(i):
+        if i < nc:
+            lo, size = cpieces[i]
+            span = pl.ds(lo + size // 4 * r, size // 4 * 3)
+            return remote(cbuf.at[OWN, span], cbuf.at[D, span], d_s.at[i], d_r.at[i], up)
         return remote(part(i, OWN), part(i, D), d_s.at[i], d_r.at[i], up)
 
+    def e_copy(i):
+        lo, size = cpieces[i]
+        span = pl.ds(lo + size // 4 * 3 * r, size // 4)
+        return remote(cbuf.at[D, span], cbuf.at[D, span], e_s.at[i], e_r.at[i], x2)
+
     def x_copies(i):
-        buf, lo, near_rows, size = cut(i)
-        one, two = pl.ds(lo, near_rows), pl.ds(lo + near_rows, size - near_rows)
+        buf, one, two = cut(i)
         return (
             remote(buf.at[xl, one], buf.at[X, one], xa_s.at[i], xa_r.at[i], x1),
             remote(buf.at[xl, two], buf.at[X, two], xb_s.at[i], xb_r.at[i], x3),
@@ -161,24 +171,32 @@
 
     def arrive(i):
         d_copy(i).wait_recv()
+        if i < nc:
+            e_copy(i).start()
 
         @pl.when(is_h)
         def _():
             for copy in x_copies(i):
                 copy.start()
 
-        @pl.when(core == 1)
-        def _():
-            py_copy(i).start()
-
+        if i >= nc:
+            complete(i)
         d_copy(i).wait_send()
         if i + 3 < n:
             d_copy(i + 3).start()
-        if i + nc < n:
+        if nc <= i + nc - 1 < n:
             @pl.when(is_l)
             def _():
-                for copy in x_copies(i + nc):
+                for copy in x_copies(i + nc - 1):
                     copy.start()
+
+    def complete(i):
+        if i < nc:
+            e_copy(i).wait_recv()
+
+        @pl.when(core == 1)
+        def _():
+            py_copy(i).start()
 
     def spread(i):
         for copy in x_copies(i):
@@ -290,13 +308,16 @@
     def in_range(j):
         return 0 <= j < nw
 
-    for i in range(nc):
-        arrive(i)
-        scores(D, *cpieces[i])
-        spread(i)
-        ready(i)
-        for slot in (X, PY, PX):
-            scores(slot, *cpieces[i])
+    for i in range(nc + 1):
+        if i < nc:
+            arrive(i)
+        if i > 0:
+            complete(i - 1)
+            spread(i - 1)
+            scores(D, *cpieces[i - 1])
+            ready(i - 1)
+            for slot in (X, PY, PX):
+                scores(slot, *cpieces[i - 1])
     arrive(nc)
     for j in range(nw + 3):
         if in_range(j):
@@ -315,6 +336,8 @@
             finish(j - 3)
 
     for i in range(n):
+        if i < nc:
+            e_copy(i).wait_send()
         for copy in x_copies(i):
             copy.wait_send()
         py_copy(i).wait_send()
@@ -360,7 +383,9 @@
             pltpu.VMEM((2, n_out, n_cen), f32),
         ]
         + [pltpu.VMEM((n_out, n_cen), f32)] * 6
-        + [dma((n,))] * 10
+        + [dma((n,))] * 2
+        + [dma((nc,))] * 2
+        + [dma((n,))] * 8
         + [dma((nw,))] * 12
         + [dma((4,)), dma((2, nw))],
         compiler_params=pltpu.CompilerParams(

time: 99.1 us -> 96.4 us (0.973)
  Pallas kernels: 95 us -> 92.3 us
    pallas_call x1, Pallas kernels: 95 us -> 92.3 us  [on_device(): pl.pallas_call(functools.partial(kernel, cpieces, wpieces, sharpness, ste...]
where the time goes in v3:
time: 96.4 us; the launch traced here: 96.2 us
  Pallas kernels  92.3 us (96%)
  local copies, waits for them, and re-layouts  3.29 us (3%)
    pallas_call x1, Pallas kernels, on_device(): pl.pallas_call(functools.partial(kernel, cpieces, wpieces, sharpness, ste...  92.3 us
    unnamed x4, local copies, waits for them, and re-layouts  3.29 us

profile of v3, /device:TPU:0, one launch (start us, length us, event | category | flops | bytes accessed | tf_op | source)
XLA Modules:
  0.0 96.2 jit_solution(15721521978363823339)
XLA Ops:
  0.6 92.3 %shard_map.77 = (f32[1000,256]{1,0:T(8,128)}, f32[1000,256]{1,0:T(8,128)}) custom-call(f32[256,1024]{1,0:T(8,128)} %ex_hbm.1, f32[1000,256]{1,0:T(8,128)} %bitcast.8, s32[1,256]{1,0:T(1,128)} %bitcast.10, f32[256,1024]{1,0:T(8,128)} %cen_hbm.1, f32[1000,256]{1,0:T(8,128)} %bitcast.9, f32[1,256]{1,0:T(1,128)} %bitcast.11), custom_call_target="tpu_custom_call" | custom-call | flops 3963617280 | bytes 7168000 | tf_op jit(solution)/shard_map/pallas_call | solution.py:369
  92.9 0.0 copy-start
  92.9 2.3 %copy.10 = f32[256,1000]{0,1:T(8,128)} copy(f32[256,1000]{0,1:T(8,128)} %bitcast.7) | data formatting | bytes 2048000
  95.3 0.0 copy-done
  95.3 1.0 copy.11
Async XLA Ops:
  92.9 2.3 %copy-start = (f32[1000,256]{1,0:T(8,128)S(1)}, f32[1000,256]{1,0:T(8,128)}, u32[]{:S(2)}) copy-start(f32[1000,256]{1,0:T(8,128)} %get-tuple-element.5) | copy-start | bytes 3072004

commit v4 on v3

--- a/solution.py
+++ b/solution.py
@@ -114,13 +114,13 @@
     def d_copy(i):
         if i < nc:
             lo, size = cpieces[i]
-            span = pl.ds(lo + size // 4 * r, size // 4 * 3)
+            span = pl.ds(lo + size // 8 * 3 * r, size // 8 * 5)
             return remote(cbuf.at[OWN, span], cbuf.at[D, span], d_s.at[i], d_r.at[i], up)
         return remote(part(i, OWN), part(i, D), d_s.at[i], d_r.at[i], up)
 
     def e_copy(i):
         lo, size = cpieces[i]
-        span = pl.ds(lo + size // 4 * 3 * r, size // 4)
+        span = pl.ds(lo + size // 8 * 5 * r, size // 8 * 3)
         return remote(cbuf.at[D, span], cbuf.at[D, span], e_s.at[i], e_r.at[i], x2)
 
     def x_copies(i):
@@ -182,8 +182,8 @@
         if i >= nc:
             complete(i)
         d_copy(i).wait_send()
-        if i + 3 < n:
-            d_copy(i + 3).start()
+        if i + 4 < n:
+            d_copy(i + 4).start()
         if nc <= i + nc - 1 < n:
             @pl.when(is_l)
             def _():
@@ -286,6 +286,7 @@
     d_copy(0).start()
     d_copy(1).start()
     d_copy(2).start()
+    d_copy(3).start()
 
     @pl.when(is_l)
     def _():

time: 96.4 us -> 101 us (1.048)
  the two profiles are of different devices: /device:TPU:0 before, /device:TPU:2 now
where the time goes in v4:
time: 101 us
  Pallas kernels  97 us (96%)
  local copies, waits for them, and re-layouts  3.29 us (3%)
    pallas_call x1, Pallas kernels, on_device(): pl.pallas_call(functools.partial(kernel, cpieces, wpieces, sharpness, ste...  97 us
    unnamed x4, local copies, waits for them, and re-layouts  3.29 us

profile of v4, /device:TPU:2, one launch (start us, length us, event | category | flops | bytes accessed | tf_op | source)
XLA Modules:
  0.0 100.9 jit_solution(16303386310727570792)
XLA Ops:
  0.6 97.0 %shard_map.77 = (f32[1000,256]{1,0:T(8,128)}, f32[1000,256]{1,0:T(8,128)}) custom-call(f32[256,1024]{1,0:T(8,128)} %ex_hbm.1, f32[1000,256]{1,0:T(8,128)} %bitcast.8, s32[1,256]{1,0:T(1,128)} %bitcast.10, f32[256,1024]{1,0:T(8,128)} %cen_hbm.1, f32[1000,256]{1,0:T(8,128)} %bitcast.9, f32[1,256]{1,0:T(1,128)} %bitcast.11), custom_call_target="tpu_custom_call" | custom-call | flops 3963617280 | bytes 7168000 | tf_op jit(solution)/shard_map/pallas_call | solution.py:370
  97.6 0.0 copy-start
  97.6 2.3 %copy.10 = f32[256,1000]{0,1:T(8,128)} copy(f32[256,1000]{0,1:T(8,128)} %bitcast.7) | data formatting | bytes 2048000
  99.9 0.0 copy-done
  99.9 1.0 copy.11
Async XLA Ops:
  97.6 2.3 %copy-start = (f32[1000,256]{1,0:T(8,128)S(1)}, f32[1000,256]{1,0:T(8,128)}, u32[]{:S(2)}) copy-start(f32[1000,256]{1,0:T(8,128)} %get-tuple-element.5) | copy-start | bytes 3072004
